TPU v7x, 128 devices: a whole 4x4x4 slice. The times are simulated.
128 devices in a mesh: tm: 128 (over z, y, x, core).
Axes of the slice: x: 4, y: 4, z: 4, core: 2. Of those that a mesh axis runs over, the one named last changes fastest.
Arguments:
- wrapped: float32 [16384, 3, 512], P('tm'), may hold values from 0 to 1, as said below
- crossings: int32 [16384, 3, 512], P('tm'), may hold values from -1 to 1, as said below
- box_size: float32 [3], replicated, may hold values from 4 to 12
Outputs:
- msd: float32 [512, 128], P('tm')
Inputs may be any that keep to these rules, and one draw needn't show every extreme that they name: `wrapped`: scaled coordinates within the unit cell. per-frame crossings, one of -1, 0, 1; most entries are 0.
All inputs are finite; a program needn't handle non-finite values.
Results may differ from a plain program's by a relative error of at most 0.0003.
Values sent between devices are 32-bit elements; how exact they have to be, the bound alone decides.
No kernel may reach another device: no remote copies, remote signals or barrier semaphores. Data moves between devices by JAX's collectives and lax.ppermute only.
A program may use at most 64 MiB of HBM per device.

v0:
```python
import jax
import jax.numpy as jnp
import numpy as np
from jax import lax
from jax.experimental import pallas as pl
from jax.experimental.pallas import tpu as pltpu
from jax.sharding import PartitionSpec as P

LAGS = 128
FRAMES = 128
CHUNKS = 128
ATOMS = 512
SENT = 13
ROWS = 16
PIECES = 2
VMEM = 48 * 1024 * 1024


def split(x):
    high = x.astype(jnp.bfloat16)
    low = (x - high.astype(x.dtype)).astype(jnp.bfloat16)
    return high, low


def tables():
    t = np.arange(FRAMES)[:, None].astype(np.float64)
    f = np.arange(FRAMES)[None, :].astype(np.float64)
    angle = 2.0 * np.pi * t * (f + 0.5) / 256.0
    forward = np.concatenate([np.cos(angle), -np.sin(angle)], axis=1)
    high, low = split(forward)
    forward = np.concatenate([high, high, low])

    turn = angle.T
    weight = 2.0 / 256.0
    sign = (1.0 - 2.0 * (np.arange(128) % 2))[:, None]
    same = 2.0 * weight * (1.0 - np.cos(turn))
    real = -2.0 * weight * sign * np.sin(turn)
    imag = -2.0 * weight * sign * np.cos(turn)
    j = np.arange(128)[:, None]
    k = np.arange(128)[None, :]
    head = (j < k).astype(np.float64)
    tail = (j > 127 - k).astype(np.float64)
    high, low = split(np.concatenate([same, real, imag, head, tail]))
    return forward, np.concatenate([high, low[:384]])


def pre_kernel(wrapped_hbm, crossings_hbm, out_ref, wrapped_ref, crossings_ref, sems):
    copies = []
    for c in range(3):
        for p in range(PIECES):
            rows = pl.ds(p * (FRAMES // PIECES), FRAMES // PIECES)
            for which, (src, dst) in enumerate(
                ((crossings_hbm, crossings_ref), (wrapped_hbm, wrapped_ref))
            ):
                copy = pltpu.make_async_copy(
                    src.at[c, rows], dst.at[c, rows], sems.at[(c * PIECES + p) * 2 + which]
                )
                copy.start()
                copies.append(copy)
    row = lax.broadcasted_iota(jnp.int32, (FRAMES, FRAMES), 0)
    col = lax.broadcasted_iota(jnp.int32, (FRAMES, FRAMES), 1)
    lower = jnp.where(col <= row, 1.0, 0.0).astype(jnp.bfloat16)
    own = lax.broadcasted_iota(jnp.int32, (4, ATOMS), 1) % 4 == lax.broadcasted_iota(
        jnp.int32, (4, ATOMS), 0
    )
    means, ends = [], []
    for c in range(3):
        for copy in copies[c * 2 * PIECES : (c + 1) * 2 * PIECES]:
            copy.wait()
        steps = crossings_ref[c].astype(jnp.float32).astype(jnp.bfloat16)
        counts = jnp.dot(lower, steps, preferred_element_type=jnp.float32)
        value = wrapped_ref[c] + counts
        mean = jnp.sum(value, axis=0, keepdims=True) * (1.0 / FRAMES)
        turned = (value - mean).T
        for d in range(CHUNKS):
            out_ref[SENT * d + 4 * c : SENT * d + 4 * c + 4, :] = turned[4 * d : 4 * d + 4]
        means.append(jnp.where(own, mean, 0.0))
        ends.append(jnp.where(own, counts[FRAMES - 1 : FRAMES] - mean, 0.0))
    blank = jnp.zeros((4, ATOMS), jnp.float32)
    notes = jnp.concatenate(means + [blank] + ends + [blank] * 25, axis=0)
    pick = jnp.where(
        lax.broadcasted_iota(jnp.int32, (CHUNKS, ATOMS), 1) // 4
        == lax.broadcasted_iota(jnp.int32, (CHUNKS, ATOMS), 0),
        1.0,
        0.0,
    ).astype(jnp.bfloat16)
    sent = jnp.zeros((CHUNKS, 128), jnp.float32)
    for _ in range(3):
        top = notes.astype(jnp.bfloat16)
        notes = notes - top.astype(jnp.float32)
        sent = sent + lax.dot_general(
            pick, top, (((1,), (1,)), ((), ())), preferred_element_type=jnp.float32
        )
    out_ref[pl.ds(SENT - 1, CHUNKS, stride=SENT), :] = sent


def post_kernel(x_ref, forward_ref, back_ref, box_ref, out_ref, wide_ref, real_ref, imag_ref):
    here = x_ref[pl.ds(SENT - 1, CHUNKS, stride=SENT), :]
    after = x_ref[pl.ds(2 * SENT - 1, CHUNKS - 1, stride=SENT), :]
    after = jnp.concatenate([after, jnp.zeros((1, 128), jnp.float32)], axis=0)
    ends = jnp.concatenate([here[:, 16:], here[:, :16]], axis=1)
    chunk = lax.broadcasted_iota(jnp.int32, (CHUNKS, 128), 0)
    gaps = jnp.where(chunk < CHUNKS - 1, after + ends, 0.0).T[0:ROWS]

    for d in range(CHUNKS):
        rows = ROWS if d < CHUNKS - 1 else SENT
        wide_ref[ROWS * d : ROWS * d + rows, :] = x_ref[SENT * d : SENT * d + rows, :]
    wide_ref[ROWS * CHUNKS - 3 : ROWS * CHUNKS, :] = jnp.zeros((3, 128), jnp.float32)
    for g in range(8):
        rows = slice(256 * g, 256 * g + 256)
        top, rest = split(wide_ref[rows, :])
        spec = jnp.dot(
            jnp.concatenate([top, rest, top], axis=1),
            forward_ref[...],
            preferred_element_type=jnp.float32,
        )
        real_ref[rows, :] = spec[:, :128]
        imag_ref[rows, :] = spec[:, 128:]

    zero = jnp.zeros((ROWS, 128), jnp.float32)
    same = both_r = both_i = za = zb = zero
    block = slice(0, ROWS)
    here_r, here_i, here_x = real_ref[block, :], imag_ref[block, :], wide_ref[block, :]
    for d in range(CHUNKS):
        same = same + (here_r * here_r + here_i * here_i)
        if d == CHUNKS - 1:
            break
        block = slice(ROWS * (d + 1), ROWS * (d + 2))
        next_r, next_i, next_x = real_ref[block, :], imag_ref[block, :], wide_ref[block, :]
        both_r = both_r + (here_r * next_r + here_i * next_i)
        both_i = both_i + (here_r * next_i - here_i * next_r)
        gap = jnp.broadcast_to(gaps[:, d : d + 1], (ROWS, 128))
        za = za + gap * here_x
        zb = zb + gap * next_x
        here_r, here_i, here_x = next_r, next_i, next_x
    first_x = wide_ref[0:ROWS, :]

    parts = jnp.concatenate(
        [
            same,
            both_r,
            both_i,
            2.0 * zb - first_x * first_x,
            -2.0 * za - here_x * here_x,
        ],
        axis=1,
    )
    top, rest = split(parts)
    sums = jnp.dot(top, back_ref[0:640, :], preferred_element_type=jnp.float32)
    sums += jnp.dot(rest, back_ref[0:640, :], preferred_element_type=jnp.float32)
    sums += jnp.dot(top[:, :384], back_ref[640:1024, :], preferred_element_type=jnp.float32)
    lags = lax.broadcasted_iota(jnp.int32, (ROWS, 128), 1).astype(jnp.float32)
    sums = sums + jnp.sum(gaps * gaps, axis=1, keepdims=True) * lags
    total = jnp.zeros((4, 128), jnp.float32)
    for c in range(3):
        total = total + sums[4 * c : 4 * c + 4] * (box_ref[c] * box_ref[c])
    out_ref[...] = total / (FRAMES * CHUNKS - lags[0:4])


def on_device(wrapped, crossings, box_size):
    forward, backward = tables()
    params = pltpu.CompilerParams(vmem_limit_bytes=VMEM)
    whole = pl.BlockSpec(memory_space=pltpu.VMEM)
    apart = pl.BlockSpec(memory_space=pltpu.HBM)
    blocks = pl.pallas_call(
        pre_kernel,
        out_shape=jax.ShapeDtypeStruct((CHUNKS * SENT, FRAMES), jnp.float32),
        in_specs=[apart, apart],
        out_specs=whole,
        scratch_shapes=[
            pltpu.VMEM((3, FRAMES, ATOMS), jnp.float32),
            pltpu.VMEM((3, FRAMES, ATOMS), jnp.int32),
            pltpu.SemaphoreType.DMA((3 * PIECES * 2,)),
        ],
        compiler_params=params,
    )(jnp.transpose(wrapped, (1, 0, 2)), jnp.transpose(crossings, (1, 0, 2)))
    mine = lax.all_to_all(
        blocks.reshape(CHUNKS * SENT, 1, FRAMES), "tm", split_axis=0, concat_axis=0, tiled=True
    )
    return pl.pallas_call(
        post_kernel,
        out_shape=jax.ShapeDtypeStruct((4, LAGS), jnp.float32),
        in_specs=[whole, whole, whole, pl.BlockSpec(memory_space=pltpu.SMEM)],
        out_specs=whole,
        scratch_shapes=[pltpu.VMEM((CHUNKS * ROWS, 128), jnp.float32)] * 3,
        compiler_params=params,
    )(
        mine.reshape(CHUNKS * SENT, FRAMES),
        jnp.asarray(forward),
        jnp.asarray(backward),
        box_size,
    )


def solution(mesh):
    in_specs = (P("tm", None, None), P("tm", None, None), P())
    return jax.shard_map(
        on_device, mesh=mesh, in_specs=in_specs, out_specs=P("tm", None), check_vma=False
    )
```

profile of v0, /device:TPU:1, one launch (start us, length us, event | category | flops | bytes accessed | tf_op | source)
XLA Modules:
  0.0 37.1 jit_solution(10739734154330068521)
XLA Ops:
  0.0 0.0 copy-start
  0.0 1.1 %copy-done = f32[128,3,512]{2,0,1:T(8,128)S(1)} copy-done((f32[128,3,512]{2,0,1:T(8,128)S(1)}, f32[128,3,512]{2,0,1:T(8,128)}, u32[]{:S(2)}) %copy-start) | copy-done | bytes 786456
  1.1 0.0 copy-start.1
  1.1 1.1 %copy-done.1 = s32[128,3,512]{2,0,1:T(8,128)S(1)} copy-done((s32[128,3,512]{2,0,1:T(8,128)S(1)}, s32[128,3,512]{2,0,1:T(8,128)}, u32[]{:S(2)}) %copy-start.1) | copy-done | bytes 786456
  2.3 3.3 %shard_map.55 = f32[1664,128]{1,0:T(8,128)S(1)} custom-call(f32[3,128,512]{2,1,0:T(8,128)S(1)} %bitcast.8, s32[3,128,512]{2,1,0:T(8,128)S(1)} %bitcast.9), custom_call_target="tpu_custom_call" | custom-call | tf_op jit(solution)/shard_map/pallas_call | solution.py:165
  5.6 0.0 copy-start.2
  5.6 0.0 copy-start.3
  5.6 28.5 %all_to_all.5 = f32[1664,1,128]{2,1,0:T(1,128)S(1)} all-to-all(f32[1664,1,128]{2,1,0:T(1,128)S(1)} %bitcast.7), channel_id=1, replica_groups=mesh['tm'=128] {'tm'}, dimensions={0} | all-to-all | bytes 1703936 | tf_op jit(solution)/shard_map/all_to_all | solution.py:177
  34.1 0.0 copy-start.4
  34.1 0.0 copy-done.2
  34.1 0.0 copy-done.3
  34.1 0.6 %copy-done.4 = f32[3]{0:T(128)S(1)} copy-done((f32[3]{0:T(128)S(1)}, f32[3]{0:T(128)}, u32[]{:S(2)}) %copy-start.4) | copy-done | bytes 36
  34.8 2.3 %shard_map.56 = f32[4,128]{1,0:T(4,128)} custom-call(f32[1664,128]{1,0:T(8,128)S(1)} %bitcast.6, bf16[384,256]{1,0:T(8,128)(2,1)S(1)} %copy-done.3, bf16[1024,128]{1,0:T(8,128)(2,1)S(1)} %copy-done.2, f32[3]{0:T(128)S(1)} %copy-done.4), custom_call_target="tpu_custom_call" | custom-call | tf_op jit(solution)/shard_map/pallas_call | solution.py:180
Async XLA Ops:
  0.0 1.1 %copy-start = (f32[128,3,512]{2,0,1:T(8,128)S(1)}, f32[128,3,512]{2,0,1:T(8,128)}, u32[]{:S(2)}) copy-start(f32[128,3,512]{2,0,1:T(8,128)} %param.5) | copy-start | bytes 2359300
  1.1 1.1 %copy-start.1 = (s32[128,3,512]{2,0,1:T(8,128)S(1)}, s32[128,3,512]{2,0,1:T(8,128)}, u32[]{:S(2)}) copy-start(s32[128,3,512]{2,0,1:T(8,128)} %param.6) | copy-start | bytes 2359300
  5.6 28.6 %copy-start.2 = (bf16[1024,128]{1,0:T(8,128)(2,1)S(1)}, bf16[1024,128]{1,0:T(8,128)(2,1)}, u32[]{:S(2)}) copy-start(bf16[1024,128]{1,0:T(8,128)(2,1)} %constant.5.clone.back_ref) | copy-start | bytes 786436
  5.6 28.6 %copy-start.3 = (bf16[384,256]{1,0:T(8,128)(2,1)S(1)}, bf16[384,256]{1,0:T(8,128)(2,1)}, u32[]{:S(2)}) copy-start(bf16[384,256]{1,0:T(8,128)(2,1)} %constant.4.clone.forward_ref) | copy-start | bytes 589828
  34.1 0.7 %copy-start.4 = (f32[3]{0:T(128)S(1)}, f32[3]{0:T(128)}, u32[]{:S(2)}) copy-start(f32[3]{0:T(128)} %box_ref.1) | copy-start | bytes 40
where the time goes:
time: 37.3 us; the launch traced here: 37.1 us
  blocking collectives  28.5 us (76%)
  Pallas kernels  5.57 us (15%)
  local copies, waits for them, and re-layouts  2.93 us (8%)
    all_to_all x1, blocking collectives, on_device(): lax.all_to_all(blocks.reshape(CHUNKS * SENT, 1, FRAMES), 'tm', split_axis...  28.5 us
    pallas_call x1, Pallas kernels, on_device(): pl.pallas_call(pre_kernel, out_shape=jax.ShapeDtypeStruct((CHUNKS * SENT,...  3.28 us
    unnamed x10, local copies, waits for them, and re-layouts  2.93 us
    pallas_call x1, Pallas kernels, on_device(): pl.pallas_call(post_kernel, out_shape=jax.ShapeDtypeStruct((4, LAGS), jnp...  2.29 us

commit v1 on v0

--- a/solution.py
+++ b/solution.py
@@ -94,7 +94,11 @@
     out_ref[pl.ds(SENT - 1, CHUNKS, stride=SENT), :] = sent
 
 
-def post_kernel(x_ref, forward_ref, back_ref, box_ref, out_ref, wide_ref, real_ref, imag_ref):
+def post_kernel(
+    x_ref, forward_ref, back_ref, box_hbm, out_ref, wide_ref, real_ref, imag_ref, box_ref, sem
+):
+    box_copy = pltpu.make_async_copy(box_hbm, box_ref, sem)
+    box_copy.start()
     here = x_ref[pl.ds(SENT - 1, CHUNKS, stride=SENT), :]
     after = x_ref[pl.ds(2 * SENT - 1, CHUNKS - 1, stride=SENT), :]
     after = jnp.concatenate([after, jnp.zeros((1, 128), jnp.float32)], axis=0)
@@ -151,10 +155,15 @@
     sums += jnp.dot(top[:, :384], back_ref[640:1024, :], preferred_element_type=jnp.float32)
     lags = lax.broadcasted_iota(jnp.int32, (ROWS, 128), 1).astype(jnp.float32)
     sums = sums + jnp.sum(gaps * gaps, axis=1, keepdims=True) * lags
+    box_copy.wait()
     total = jnp.zeros((4, 128), jnp.float32)
     for c in range(3):
         total = total + sums[4 * c : 4 * c + 4] * (box_ref[c] * box_ref[c])
     out_ref[...] = total / (FRAMES * CHUNKS - lags[0:4])
+
+
+def in_hbm(x):
+    return pltpu.with_memory_space_constraint(x, pltpu.HBM)
 
 
 def on_device(wrapped, crossings, box_size):
@@ -173,22 +182,23 @@
             pltpu.SemaphoreType.DMA((3 * PIECES * 2,)),
         ],
         compiler_params=params,
-    )(jnp.transpose(wrapped, (1, 0, 2)), jnp.transpose(crossings, (1, 0, 2)))
+    )(in_hbm(jnp.transpose(wrapped, (1, 0, 2))), in_hbm(jnp.transpose(crossings, (1, 0, 2))))
     mine = lax.all_to_all(
         blocks.reshape(CHUNKS * SENT, 1, FRAMES), "tm", split_axis=0, concat_axis=0, tiled=True
     )
     return pl.pallas_call(
         post_kernel,
         out_shape=jax.ShapeDtypeStruct((4, LAGS), jnp.float32),
-        in_specs=[whole, whole, whole, pl.BlockSpec(memory_space=pltpu.SMEM)],
+        in_specs=[whole, whole, whole, apart],
         out_specs=whole,
-        scratch_shapes=[pltpu.VMEM((CHUNKS * ROWS, 128), jnp.float32)] * 3,
+        scratch_shapes=[pltpu.VMEM((CHUNKS * ROWS, 128), jnp.float32)] * 3
+        + [pltpu.SMEM((3,), jnp.float32), pltpu.SemaphoreType.DMA],
         compiler_params=params,
     )(
         mine.reshape(CHUNKS * SENT, FRAMES),
         jnp.asarray(forward),
         jnp.asarray(backward),
-        box_size,
+        in_hbm(box_size),
     )
 
 

time: 37.3 us -> 32.9 us (0.88)
  local copies, waits for them, and re-layouts: 2.93 us -> 0.01 us
  Pallas kernels: 5.57 us -> 4.15 us
    unnamed x10 -> x4, local copies, waits for them, and re-layouts: 2.93 us -> 0.01 us
    pallas_call x1, Pallas kernels: 3.28 us -> 2.36 us  [on_device(): pl.pallas_call(pre_kernel, out_shape=jax.ShapeDtypeStruct((CHUNKS * SENT,...]
    pallas_call x1, Pallas kernels: 2.29 us -> 1.79 us  [on_device(): pl.pallas_call(post_kernel, out_shape=jax.ShapeDtypeStruct((4, LAGS), jnp...]
where the time goes in v1:
time: 32.9 us; the launch traced here: 32.7 us
  blocking collectives  28.5 us (87%)
  Pallas kernels  4.15 us (13%)
    all_to_all x1, blocking collectives, on_device(): lax.all_to_all(blocks.reshape(CHUNKS * SENT, 1, FRAMES), 'tm', split_axis...  28.5 us
    pallas_call x1, Pallas kernels, on_device(): pl.pallas_call(pre_kernel, out_shape=jax.ShapeDtypeStruct((CHUNKS * SENT,...  2.36 us
    pallas_call x1, Pallas kernels, on_device(): pl.pallas_call(post_kernel, out_shape=jax.ShapeDtypeStruct((4, LAGS), jnp...  1.79 us

profile of v1, /device:TPU:1, one launch (start us, length us, event | category | flops | bytes accessed | tf_op | source)
XLA Modules:
  0.0 32.7 jit_solution(2515656023730470249)
XLA Ops:
  0.0 2.4 %shard_map.55 = f32[1664,128]{1,0:T(8,128)S(1)} custom-call(f32[3,128,512]{2,1,0:T(8,128)} %bitcast.8, s32[3,128,512]{2,1,0:T(8,128)} %bitcast.9), custom_call_target="tpu_custom_call" | custom-call | tf_op jit(solution)/shard_map/pallas_call | solution.py:174
  2.4 0.0 copy-start
  2.4 0.0 copy-start.1
  2.4 28.5 %all_to_all.5 = f32[1664,1,128]{2,1,0:T(1,128)S(1)} all-to-all(f32[1664,1,128]{2,1,0:T(1,128)S(1)} %bitcast.7), channel_id=1, replica_groups=mesh['tm'=128] {'tm'}, dimensions={0} | all-to-all | bytes 1703936 | tf_op jit(solution)/shard_map/all_to_all | solution.py:186
  30.9 0.0 copy-done
  30.9 0.0 copy-done.1
  30.9 1.8 %shard_map.56 = f32[4,128]{1,0:T(4,128)} custom-call(f32[1664,128]{1,0:T(8,128)S(1)} %bitcast.6, bf16[384,256]{1,0:T(8,128)(2,1)S(1)} %copy-done.1, bf16[1024,128]{1,0:T(8,128)(2,1)S(1)} %copy-done, f32[3]{0:T(128)} %box_hbm.1), custom_call_target="tpu_custom_call" | custom-call | tf_op jit(solution)/shard_map/pallas_call | solution.py:189
Async XLA Ops:
  2.4 28.6 %copy-start = (bf16[1024,128]{1,0:T(8,128)(2,1)S(1)}, bf16[1024,128]{1,0:T(8,128)(2,1)}, u32[]{:S(2)}) copy-start(bf16[1024,128]{1,0:T(8,128)(2,1)} %constant.5.clone.back_ref) | copy-start | bytes 786436
  2.4 28.6 %copy-start.1 = (bf16[384,256]{1,0:T(8,128)(2,1)S(1)}, bf16[384,256]{1,0:T(8,128)(2,1)}, u32[]{:S(2)}) copy-start(bf16[384,256]{1,0:T(8,128)(2,1)} %constant.4.clone.forward_ref) | copy-start | bytes 589828

commit v2 on v1

--- a/solution.py
+++ b/solution.py
@@ -12,8 +12,9 @@
 ATOMS = 512
 SENT = 13
 ROWS = 16
-PIECES = 2
 VMEM = 48 * 1024 * 1024
+ORDER = [d for j in range(CHUNKS // 2) for d in (CHUNKS - 1 - j, j)]
+PLACE = [ORDER.index(d) for d in range(CHUNKS)]
 
 
 def split(x):
@@ -47,43 +48,40 @@
 def pre_kernel(wrapped_hbm, crossings_hbm, out_ref, wrapped_ref, crossings_ref, sems):
     copies = []
     for c in range(3):
-        for p in range(PIECES):
-            rows = pl.ds(p * (FRAMES // PIECES), FRAMES // PIECES)
-            for which, (src, dst) in enumerate(
-                ((crossings_hbm, crossings_ref), (wrapped_hbm, wrapped_ref))
-            ):
-                copy = pltpu.make_async_copy(
-                    src.at[c, rows], dst.at[c, rows], sems.at[(c * PIECES + p) * 2 + which]
-                )
-                copy.start()
-                copies.append(copy)
+        for src, dst in ((crossings_hbm, crossings_ref), (wrapped_hbm, wrapped_ref)):
+            copy = pltpu.make_async_copy(src.at[c], dst.at[c], sems.at[len(copies)])
+            copy.start()
+            copies.append(copy)
     row = lax.broadcasted_iota(jnp.int32, (FRAMES, FRAMES), 0)
     col = lax.broadcasted_iota(jnp.int32, (FRAMES, FRAMES), 1)
-    lower = jnp.where(col <= row, 1.0, 0.0).astype(jnp.bfloat16)
+    upper = jnp.where(row <= col, 1.0, 0.0).astype(jnp.bfloat16)
     own = lax.broadcasted_iota(jnp.int32, (4, ATOMS), 1) % 4 == lax.broadcasted_iota(
         jnp.int32, (4, ATOMS), 0
     )
+    place = lax.broadcasted_iota(jnp.int32, (CHUNKS, ATOMS), 0)
+    owner = jnp.where(place % 2 == 0, CHUNKS - 1 - place // 2, place // 2)
+    pick = jnp.where(
+        lax.broadcasted_iota(jnp.int32, (CHUNKS, ATOMS), 1) // 4 == owner, 1.0, 0.0
+    ).astype(jnp.bfloat16)
     means, ends = [], []
     for c in range(3):
-        for copy in copies[c * 2 * PIECES : (c + 1) * 2 * PIECES]:
+        for copy in copies[2 * c : 2 * c + 2]:
             copy.wait()
         steps = crossings_ref[c].astype(jnp.float32).astype(jnp.bfloat16)
-        counts = jnp.dot(lower, steps, preferred_element_type=jnp.float32)
-        value = wrapped_ref[c] + counts
-        mean = jnp.sum(value, axis=0, keepdims=True) * (1.0 / FRAMES)
-        turned = (value - mean).T
+        moves = crossings_ref[c].astype(jnp.float32)
+        left = (FRAMES - lax.broadcasted_iota(jnp.int32, (FRAMES, 1), 0)).astype(jnp.float32)
+        mean = jnp.sum(wrapped_ref[c] + moves * left, axis=0, keepdims=True) * (1.0 / FRAMES)
+        end = jnp.sum(moves, axis=0, keepdims=True)
+        turned = (wrapped_ref[c] - mean).T + lax.dot_general(
+            steps, upper, (((0,), (0,)), ((), ())), preferred_element_type=jnp.float32
+        )
         for d in range(CHUNKS):
-            out_ref[SENT * d + 4 * c : SENT * d + 4 * c + 4, :] = turned[4 * d : 4 * d + 4]
+            start = SENT * PLACE[d] + 4 * c
+            out_ref[start : start + 4, :] = turned[4 * d : 4 * d + 4]
         means.append(jnp.where(own, mean, 0.0))
-        ends.append(jnp.where(own, counts[FRAMES - 1 : FRAMES] - mean, 0.0))
+        ends.append(jnp.where(own, end - mean, 0.0))
     blank = jnp.zeros((4, ATOMS), jnp.float32)
     notes = jnp.concatenate(means + [blank] + ends + [blank] * 25, axis=0)
-    pick = jnp.where(
-        lax.broadcasted_iota(jnp.int32, (CHUNKS, ATOMS), 1) // 4
-        == lax.broadcasted_iota(jnp.int32, (CHUNKS, ATOMS), 0),
-        1.0,
-        0.0,
-    ).astype(jnp.bfloat16)
     sent = jnp.zeros((CHUNKS, 128), jnp.float32)
     for _ in range(3):
         top = notes.astype(jnp.bfloat16)
@@ -99,17 +97,20 @@
 ):
     box_copy = pltpu.make_async_copy(box_hbm, box_ref, sem)
     box_copy.start()
-    here = x_ref[pl.ds(SENT - 1, CHUNKS, stride=SENT), :]
-    after = x_ref[pl.ds(2 * SENT - 1, CHUNKS - 1, stride=SENT), :]
+    for d in range(CHUNKS):
+        rows = ROWS if PLACE[d] < CHUNKS - 1 else SENT
+        start = SENT * PLACE[d]
+        wide_ref[ROWS * d : ROWS * d + rows, :] = x_ref[start : start + rows, :]
+        if rows < ROWS:
+            wide_ref[ROWS * d + rows : ROWS * d + ROWS, :] = jnp.zeros((ROWS - rows, 128), jnp.float32)
+
+    here = wide_ref[pl.ds(SENT - 1, CHUNKS, stride=ROWS), :]
+    after = wide_ref[pl.ds(ROWS + SENT - 1, CHUNKS - 1, stride=ROWS), :]
     after = jnp.concatenate([after, jnp.zeros((1, 128), jnp.float32)], axis=0)
     ends = jnp.concatenate([here[:, 16:], here[:, :16]], axis=1)
     chunk = lax.broadcasted_iota(jnp.int32, (CHUNKS, 128), 0)
     gaps = jnp.where(chunk < CHUNKS - 1, after + ends, 0.0).T[0:ROWS]
 
-    for d in range(CHUNKS):
-        rows = ROWS if d < CHUNKS - 1 else SENT
-        wide_ref[ROWS * d : ROWS * d + rows, :] = x_ref[SENT * d : SENT * d + rows, :]
-    wide_ref[ROWS * CHUNKS - 3 : ROWS * CHUNKS, :] = jnp.zeros((3, 128), jnp.float32)
     for g in range(8):
         rows = slice(256 * g, 256 * g + 256)
         top, rest = split(wide_ref[rows, :])
@@ -179,12 +180,17 @@
         scratch_shapes=[
             pltpu.VMEM((3, FRAMES, ATOMS), jnp.float32),
             pltpu.VMEM((3, FRAMES, ATOMS), jnp.int32),
-            pltpu.SemaphoreType.DMA((3 * PIECES * 2,)),
+            pltpu.SemaphoreType.DMA((6,)),
         ],
         compiler_params=params,
     )(in_hbm(jnp.transpose(wrapped, (1, 0, 2))), in_hbm(jnp.transpose(crossings, (1, 0, 2))))
     mine = lax.all_to_all(
-        blocks.reshape(CHUNKS * SENT, 1, FRAMES), "tm", split_axis=0, concat_axis=0, tiled=True
+        blocks.reshape(CHUNKS * SENT, 1, FRAMES),
+        "tm",
+        split_axis=0,
+        concat_axis=0,
+        tiled=True,
+        axis_index_groups=[ORDER],
     )
     return pl.pallas_call(
         post_kernel,

time: 32.9 us -> 31.4 us (0.954)
  blocking collectives: 28.5 us -> 27.4 us
  Pallas kernels: 4.15 us -> 3.75 us
    all_to_all x1, blocking collectives: 28.5 us -> 27.4 us  [on_device(): lax.all_to_all(blocks.reshape(CHUNKS * SENT, 1, FRAMES), 'tm', split_axis...]
    pallas_call x1, Pallas kernels: 2.36 us -> 1.98 us  [on_device(): pl.pallas_call(pre_kernel, out_shape=jax.ShapeDtypeStruct((CHUNKS * SENT,...]
where the time goes in v2:
time: 31.4 us; the launch traced here: 31.2 us
  blocking collectives  27.4 us (87%)
  Pallas kernels  3.75 us (12%)
    all_to_all x1, blocking collectives, on_device(): lax.all_to_all(blocks.reshape(CHUNKS * SENT, 1, FRAMES), 'tm', split_axis...  27.4 us
    pallas_call x1, Pallas kernels, on_device(): pl.pallas_call(pre_kernel, out_shape=jax.ShapeDtypeStruct((CHUNKS * SENT,...  1.98 us
    pallas_call x1, Pallas kernels, on_device(): pl.pallas_call(post_kernel, out_shape=jax.ShapeDtypeStruct((4, LAGS), jnp...  1.78 us

profile of v2, /device:TPU:1, one launch (start us, length us, event | category | flops | bytes accessed | tf_op | source)
XLA Modules:
  0.0 31.2 jit_solution(724953800150546841)
XLA Ops:
  0.0 2.0 %shard_map.55 = f32[1664,128]{1,0:T(8,128)S(1)} custom-call(f32[3,128,512]{2,1,0:T(8,128)} %bitcast.8, s32[3,128,512]{2,1,0:T(8,128)} %bitcast.9), custom_call_target="tpu_custom_call" | custom-call | tf_op jit(solution)/shard_map/pallas_call | solution.py:175
  2.0 0.0 copy-start
  2.0 0.0 copy-start.1
  2.0 27.4 %all_to_all.5 = f32[1664,1,128]{2,1,0:T(1,128)S(1)} all-to-all(f32[1664,1,128]{2,1,0:T(1,128)S(1)} %bitcast.7), channel_id=1, replica_groups={{127,0,126,1,125,2,124,3,123,4,122,5,121,6,120,7,119,8,118,9,117,10,116..., dimensions={0} | all-to-all | bytes 1703936 | tf_op jit(solution)/shard_map/all_to_all | solution.py:187
  29.4 0.0 copy-done
  29.4 0.0 copy-done.1
  29.5 1.8 %shard_map.56 = f32[4,128]{1,0:T(4,128)} custom-call(f32[1664,128]{1,0:T(8,128)S(1)} %bitcast.6, bf16[384,256]{1,0:T(8,128)(2,1)S(1)} %copy-done.1, bf16[1024,128]{1,0:T(8,128)(2,1)S(1)} %copy-done, f32[3]{0:T(128)} %box_hbm.1), custom_call_target="tpu_custom_call" | custom-call | tf_op jit(solution)/shard_map/pallas_call | solution.py:195
Async XLA Ops:
  2.0 27.5 %copy-start = (bf16[1024,128]{1,0:T(8,128)(2,1)S(1)}, bf16[1024,128]{1,0:T(8,128)(2,1)}, u32[]{:S(2)}) copy-start(bf16[1024,128]{1,0:T(8,128)(2,1)} %constant.5.clone.back_ref) | copy-start | bytes 786436
  2.0 27.5 %copy-start.1 = (bf16[384,256]{1,0:T(8,128)(2,1)S(1)}, bf16[384,256]{1,0:T(8,128)(2,1)}, u32[]{:S(2)}) copy-start(bf16[384,256]{1,0:T(8,128)(2,1)} %constant.4.clone.forward_ref) | copy-start | bytes 589828

commit v3 on v2

--- a/solution.py
+++ b/solution.py
@@ -13,7 +13,7 @@
 SENT = 13
 ROWS = 16
 VMEM = 48 * 1024 * 1024
-ORDER = [d for j in range(CHUNKS // 2) for d in (CHUNKS - 1 - j, j)]
+ORDER = [d for j in range(CHUNKS // 2) for d in (CHUNKS - 1 - j, j ^ 1)]
 PLACE = [ORDER.index(d) for d in range(CHUNKS)]
 
 
@@ -59,7 +59,8 @@
         jnp.int32, (4, ATOMS), 0
     )
     place = lax.broadcasted_iota(jnp.int32, (CHUNKS, ATOMS), 0)
-    owner = jnp.where(place % 2 == 0, CHUNKS - 1 - place // 2, place // 2)
+    pair = place // 2
+    owner = jnp.where(place % 2 == 0, CHUNKS - 1 - pair, pair + 1 - 2 * (pair % 2))
     pick = jnp.where(
         lax.broadcasted_iota(jnp.int32, (CHUNKS, ATOMS), 1) // 4 == owner, 1.0, 0.0
     ).astype(jnp.bfloat16)

time: 31.4 us -> 30.9 us (0.984)
  blocking collectives: 27.4 us -> 26.9 us
    all_to_all x1, blocking collectives: 27.4 us -> 26.9 us  [on_device(): lax.all_to_all(blocks.reshape(CHUNKS * SENT, 1, FRAMES), 'tm', split_axis...]
where the time goes in v3:
time: 30.9 us; the launch traced here: 30.7 us
  blocking collectives  26.9 us (87%)
  Pallas kernels  3.75 us (12%)
    all_to_all x1, blocking collectives, on_device(): lax.all_to_all(blocks.reshape(CHUNKS * SENT, 1, FRAMES), 'tm', split_axis...  26.9 us
    pallas_call x1, Pallas kernels, on_device(): pl.pallas_call(pre_kernel, out_shape=jax.ShapeDtypeStruct((CHUNKS * SENT,...  1.97 us
    pallas_call x1, Pallas kernels, on_device(): pl.pallas_call(post_kernel, out_shape=jax.ShapeDtypeStruct((4, LAGS), jnp...  1.78 us

profile of v3, /device:TPU:1, one launch (start us, length us, event | category | flops | bytes accessed | tf_op | source)
XLA Modules:
  0.0 30.7 jit_solution(7319014883488670174)
XLA Ops:
  0.0 2.0 %shard_map.55 = f32[1664,128]{1,0:T(8,128)S(1)} custom-call(f32[3,128,512]{2,1,0:T(8,128)} %bitcast.8, s32[3,128,512]{2,1,0:T(8,128)} %bitcast.9), custom_call_target="tpu_custom_call" | custom-call | tf_op jit(solution)/shard_map/pallas_call | solution.py:176
  2.0 0.0 copy-start
  2.0 0.0 copy-start.1
  2.0 26.9 %all_to_all.5 = f32[1664,1,128]{2,1,0:T(1,128)S(1)} all-to-all(f32[1664,1,128]{2,1,0:T(1,128)S(1)} %bitcast.7), channel_id=1, replica_groups={{127,1,126,0,125,3,124,2,123,5,122,4,121,7,120,6,119,9,118,8,117,11,116..., dimensions={0} | all-to-all | bytes 1703936 | tf_op jit(solution)/shard_map/all_to_all | solution.py:188
  28.9 0.0 copy-done
  28.9 0.0 copy-done.1
  28.9 1.8 %shard_map.56 = f32[4,128]{1,0:T(4,128)} custom-call(f32[1664,128]{1,0:T(8,128)S(1)} %bitcast.6, bf16[384,256]{1,0:T(8,128)(2,1)S(1)} %copy-done.1, bf16[1024,128]{1,0:T(8,128)(2,1)S(1)} %copy-done, f32[3]{0:T(128)} %box_hbm.1), custom_call_target="tpu_custom_call" | custom-call | tf_op jit(solution)/shard_map/pallas_call | solution.py:196
Async XLA Ops:
  2.0 26.9 %copy-start = (bf16[1024,128]{1,0:T(8,128)(2,1)S(1)}, bf16[1024,128]{1,0:T(8,128)(2,1)}, u32[]{:S(2)}) copy-start(bf16[1024,128]{1,0:T(8,128)(2,1)} %constant.5.clone.back_ref) | copy-start | bytes 786436
  2.0 26.9 %copy-start.1 = (bf16[384,256]{1,0:T(8,128)(2,1)S(1)}, bf16[384,256]{1,0:T(8,128)(2,1)}, u32[]{:S(2)}) copy-start(bf16[384,256]{1,0:T(8,128)(2,1)} %constant.4.clone.forward_ref) | copy-start | bytes 589828

commit v4 on v3

--- a/solution.py
+++ b/solution.py
@@ -65,9 +65,9 @@
         lax.broadcasted_iota(jnp.int32, (CHUNKS, ATOMS), 1) // 4 == owner, 1.0, 0.0
     ).astype(jnp.bfloat16)
     means, ends = [], []
+    for copy in copies:
+        copy.wait()
     for c in range(3):
-        for copy in copies[2 * c : 2 * c + 2]:
-            copy.wait()
         steps = crossings_ref[c].astype(jnp.float32).astype(jnp.bfloat16)
         moves = crossings_ref[c].astype(jnp.float32)
         left = (FRAMES - lax.broadcasted_iota(jnp.int32, (FRAMES, 1), 0)).astype(jnp.float32)

time: 30.9 us -> 30.9 us (level)
  no operation moved by 1% of the time
where the time goes in v4:
time: 30.9 us; the launch traced here: 30.6 us
  blocking collectives  26.9 us (87%)
  Pallas kernels  3.71 us (12%)
    all_to_all x1, blocking collectives, on_device(): lax.all_to_all(blocks.reshape(CHUNKS * SENT, 1, FRAMES), 'tm', split_axis...  26.9 us
    pallas_call x1, Pallas kernels, on_device(): pl.pallas_call(pre_kernel, out_shape=jax.ShapeDtypeStruct((CHUNKS * SENT,...  1.94 us
    pallas_call x1, Pallas kernels, on_device(): pl.pallas_call(post_kernel, out_shape=jax.ShapeDtypeStruct((4, LAGS), jnp...  1.77 us

profile of v4, /device:TPU:1, one launch (start us, length us, event | category | flops | bytes accessed | tf_op | source)
XLA Modules:
  0.0 30.6 jit_solution(3420491293991314649)
XLA Ops:
  0.0 1.9 %shard_map.55 = f32[1664,128]{1,0:T(8,128)S(1)} custom-call(f32[3,128,512]{2,1,0:T(8,128)} %bitcast.8, s32[3,128,512]{2,1,0:T(8,128)} %bitcast.9), custom_call_target="tpu_custom_call" | custom-call | tf_op jit(solution)/shard_map/pallas_call | solution.py:176
  1.9 0.0 copy-start
  2.0 0.0 copy-start.1
  2.0 26.9 %all_to_all.5 = f32[1664,1,128]{2,1,0:T(1,128)S(1)} all-to-all(f32[1664,1,128]{2,1,0:T(1,128)S(1)} %bitcast.7), channel_id=1, replica_groups={{127,1,126,0,125,3,124,2,123,5,122,4,121,7,120,6,119,9,118,8,117,11,116..., dimensions={0} | all-to-all | bytes 1703936 | tf_op jit(solution)/shard_map/all_to_all | solution.py:188
  28.8 0.0 copy-done
  28.8 0.0 copy-done.1
  28.8 1.8 %shard_map.56 = f32[4,128]{1,0:T(4,128)} custom-call(f32[1664,128]{1,0:T(8,128)S(1)} %bitcast.6, bf16[384,256]{1,0:T(8,128)(2,1)S(1)} %copy-done.1, bf16[1024,128]{1,0:T(8,128)(2,1)S(1)} %copy-done, f32[3]{0:T(128)} %box_hbm.1), custom_call_target="tpu_custom_call" | custom-call | tf_op jit(solution)/shard_map/pallas_call | solution.py:196
Async XLA Ops:
  1.9 26.9 %copy-start = (bf16[1024,128]{1,0:T(8,128)(2,1)S(1)}, bf16[1024,128]{1,0:T(8,128)(2,1)}, u32[]{:S(2)}) copy-start(bf16[1024,128]{1,0:T(8,128)(2,1)} %constant.5.clone.back_ref) | copy-start | bytes 786436
  2.0 26.9 %copy-start.1 = (bf16[384,256]{1,0:T(8,128)(2,1)S(1)}, bf16[384,256]{1,0:T(8,128)(2,1)}, u32[]{:S(2)}) copy-start(bf16[384,256]{1,0:T(8,128)(2,1)} %constant.4.clone.forward_ref) | copy-start | bytes 589828
